TPU v7x, 1024 devices: a whole 8x8x8 slice. The times are simulated.
1024 devices in a mesh: dp: 8 (over x), context: 16 (over y, core), tensor: 8 (over z).
Axes of the slice: x: 8, y: 8, z: 8, core: 2. Of those that a mesh axis runs over, the one named last changes fastest.
Arguments:
- hidden: bfloat16 [32768, 4096], P(('dp', 'context')), parts along dimension 0, may hold values from -6 to 6
- expert_ids: int32 [32768, 8], P(('dp', 'context')), parts along dimension 0, may hold values from 0 to 127, all different within a row; in each aligned block of 256 rows (0 to 255, 256 to 511, ...) at most 32 rows name the same one
- gate_weights: float32 [32768, 8], P(('dp', 'context')), parts along dimension 0, may hold values from 0.2 to 1
- w_gate: bfloat16 [16, 4096, 1536], P('context', None, 'tensor'), may hold values from -0.09375 to 0.09375
- w_up: bfloat16 [16, 4096, 1536], P('context', None, 'tensor'), may hold values from -0.09375 to 0.09375
- w_down: bfloat16 [16, 1536, 4096], P('context', 'tensor'), may hold values from -0.21875 to 0.21875
Outputs:
- mixed: bfloat16 [32768, 4096], P(('dp', 'context'), 'tensor'), parts along dimension 0
There are 8 independent parts, one for each index of `dp`. A program takes and returns all parts, laid end to end along the dimension named above; an argument that names none is the same for every part. Nothing has to cross between parts.
Inputs may be any that keep to these rules, and one draw needn't show every extreme that they name: `expert_ids`: each row names 8 different experts. Among the 256 rows of one context index no expert is named by more than 32 rows, a bound that some block reaches.
All inputs are finite; a program needn't handle non-finite values.
Results may differ from a plain program's by a relative error of at most 0.02.
Values may be sent and summed in bfloat16 or wider, within the bound.
A program may use at most 64 MiB of HBM per device.

v0:
```python
import jax
import jax.numpy as jnp
from jax import lax
from jax.sharding import PartitionSpec as P

CAP = 32


def local(hidden, expert_ids, gate_weights, w_gate, w_up, w_down):
    group_count = lax.axis_size("context")
    model_width = hidden.shape[1]
    slice_width = model_width // lax.axis_size("tensor")
    experts = jnp.arange(group_count, dtype=jnp.int32)
    matches = expert_ids[:, :, None] == experts[None, None, :]
    chosen = jnp.any(matches, axis=1)
    weight = jnp.sum(jnp.where(matches, gate_weights[:, :, None], jnp.float32(0.0)), axis=1)
    position = jnp.cumsum(chosen.astype(jnp.int32), axis=0) - 1
    slot_ids = jnp.arange(CAP, dtype=jnp.int32)
    placed = jnp.logical_and(
        chosen.T[:, None, :], position.T[:, None, :] == slot_ids[None, :, None]
    )
    selector = placed.astype(jnp.bfloat16)
    outgoing = jnp.einsum(
        "est,td->esd", selector, hidden, preferred_element_type=jnp.float32
    ).astype(jnp.bfloat16)
    slot_rows = group_count * CAP
    arrived = lax.all_to_all(outgoing, "context", split_axis=0, concat_axis=0, tiled=True)
    arrived_rows = arrived.reshape(slot_rows, model_width)
    gate_acts = jnp.dot(arrived_rows, w_gate[0], preferred_element_type=jnp.float32)
    up_acts = jnp.dot(arrived_rows, w_up[0], preferred_element_type=jnp.float32)
    activated = (jax.nn.silu(gate_acts) * up_acts).astype(jnp.bfloat16)
    partial_out = jnp.dot(activated, w_down[0], preferred_element_type=jnp.float32)
    summed = lax.psum_scatter(
        partial_out.astype(jnp.bfloat16), "tensor", scatter_dimension=1, tiled=True
    )
    expert_out = summed.reshape(group_count, CAP, slice_width)
    returned = lax.all_to_all(expert_out, "context", split_axis=0, concat_axis=0, tiled=True)
    combiner = placed.astype(jnp.float32) * weight.T[:, None, :]
    combiner_high = combiner.astype(jnp.bfloat16)
    combiner_low = (combiner - combiner_high.astype(jnp.float32)).astype(jnp.bfloat16)
    totals_out = jnp.einsum(
        "est,esd->td", combiner_high, returned, preferred_element_type=jnp.float32
    )
    totals_out = totals_out + jnp.einsum(
        "est,esd->td", combiner_low, returned, preferred_element_type=jnp.float32
    )
    return totals_out.astype(jnp.bfloat16)


def solution(mesh):
    placed = (
        P(("dp", "context"), None),
        P(("dp", "context"), None),
        P(("dp", "context"), None),
        P("context", None, "tensor"),
        P("context", None, "tensor"),
        P("context", "tensor", None),
    )
    return jax.shard_map(
        local, mesh=mesh, in_specs=placed, out_specs=P(("dp", "context"), "tensor"), check_vma=False
    )
```

profile of v0, /device:TPU:1, one launch (start us, length us, event | category | flops | bytes accessed | tf_op | source)
XLA Modules:
  0.0 227.8 jit_solution(866261397709474603)
XLA Ops:
  6.5 0.0 copy-start
  6.5 0.0 reduce-scatter.2.cloned.1.call-start
  6.5 0.9 fusion.36
  7.4 0.6 reduce-window.6
  8.0 0.2 slice_reduce_fusion
  8.2 0.1 copy_bitcast_fusion
  8.3 0.0 copy-done
  8.3 1.3 convolution_convert_fusion.1
  9.6 0.0 copy-start.4
  9.6 112.8 %all_to_all.10 = bf16[16,32,4096]{2,1,0:T(8,128)(2,1)S(1)} all-to-all(bf16[16,32,4096]{2,1,0:T(8,128)(2,1)S(1)} %convolution_convert_fusion.1), channel_id=1, replica_groups=mesh['dp'=8,'context'=16,'tensor'=8] {'context'}, dimensions={0} | all-to-all | bytes 8388608 | tf_op jit(solution)/shard_map/all_to_all | solution.py:27
  122.3 0.0 copy-start.1
  122.4 2.0 copy-done.1
  124.3 0.0 copy-done.4
  124.3 1.5 fusion.4
  125.9 7.9 %convolution_convert_fusion = bf16[512,4096]{1,0:T(8,128)(2,1)} fusion(bf16[1,192,4096]{2,1,0:T(8,128)(2,1)} %param.11, bf16[512,4096]{1,0:T(8,128)(2,1)} %bitcast.47, bf16[1,4096,192]{1,2,0:T(8,128)(2,1)} %param.10, f32[512,192]{0,1:T(8,128)S(1)} %fusion.4), kind=kOutput, calls=%fused_computation | convolution fusion | flops 1613299712 | bytes 11927552 | tf_op jit(solution)/shard_map/dot_general | solution.py:32
  133.7 0.0 copy-start.2
  133.7 0.0 copy-start.3
  133.7 0.0 reduce-scatter.2.cloned.1.call-update
  133.8 61.0 %reduce-scatter.2.cloned.1.call-done = bf16[512,512]{1,0:T(8,128)(2,1)} async-done(((bf16[512,4096]{1,0:T(8,128)(2,1)}), bf16[512,512]{1,0:T(8,128)(2,1)}) %reduce-scatter.2.cloned.1.call-update) | async-done | bytes 524304 | tf_op jit(solution)/shard_map/reduce_scatter | solution.py:33
  194.8 7.5 %all-to-all-start.1 = ((bf16[16,32,512]{2,1,0:T(8,128)(2,1)}), bf16[16,32,512]{2,1,0:T(8,128)(2,1)S(1)}, u32[]{:S(2)}, u32[]{:S(2)}) async-start(bf16[16,32,512]{2,1,0:T(8,128)(2,1)} %bitcast.48), calls=%async_computation.2 | async-start | bytes 1048576 | tf_op jit(solution)/shard_map/all_to_all | solution.py:37
  202.2 0.0 copy-done.2
  202.3 0.0 copy-done.3
  202.3 17.3 %all-to-all-done.1 = bf16[16,32,512]{2,1,0:T(8,128)(2,1)S(1)} async-done(((bf16[16,32,512]{2,1,0:T(8,128)(2,1)}), bf16[16,32,512]{2,1,0:T(8,128)(2,1)S(1)}, u32[]{:S(2)}, u32[]{:S(2)}) %all-to-all-start.1) | async-done | bytes 524320 | tf_op jit(solution)/shard_map/all_to_all | solution.py:37
  219.6 0.3 convolution_bitcast_fusion
  219.9 1.0 fusion.7
  (4 shorter events, 0.1 us)
Async XLA Ops:
  6.5 1.8 copy-start
  6.5 188.3 %reduce-scatter.2.cloned.1.call-start = ((), (), s32[]{:S(2)}) async-start(), calls=%async_computation.3 | async-start | bytes 4718592 | tf_op jit(solution)/shard_map/reduce_scatter | solution.py:33
  9.6 114.7 %copy-start.4 = (bf16[1,4096,192]{1,2,0:T(8,128)(2,1)S(1)}, bf16[1,4096,192]{1,2,0:T(8,128)(2,1)}, u32[]{:S(2)}) copy-start(bf16[1,4096,192]{1,2,0:T(8,128)(2,1)} %param.9) | copy-start | bytes 4718596
  122.3 2.0 copy-start.1
  133.7 68.5 %copy-start.2 = (s32[256,8]{0,1:T(8,128)S(1)}, s32[256,8]{0,1:T(8,128)}, u32[]{:S(2)}) copy-start(s32[256,8]{0,1:T(8,128)} %param.7) | copy-start | bytes 24580
  133.7 68.5 %copy-start.3 = (f32[256,8]{0,1:T(8,128)S(1)}, f32[256,8]{0,1:T(8,128)}, u32[]{:S(2)}) copy-start(f32[256,8]{0,1:T(8,128)} %param.8) | copy-start | bytes 24580
  194.8 24.8 %all-to-all-start.1 = ((bf16[16,32,512]{2,1,0:T(8,128)(2,1)}), bf16[16,32,512]{2,1,0:T(8,128)(2,1)S(1)}, u32[]{:S(2)}, u32[]{:S(2)}) async-start(bf16[16,32,512]{2,1,0:T(8,128)(2,1)} %bitcast.48), calls=%async_computation.2 | async-start | bytes 1048576 | tf_op jit(solution)/shard_map/all_to_all | solution.py:37
Sparse Core Ops, SparseCore 0:
  133.9 60.8 reduce-scatter.1
where the time goes:
time: 228 us
  blocking collectives  113 us (50%)
  waiting for transfers between devices  78.3 us (34%)
  between operations  13.4 us (6%)
  matrix products  12 us (5%)
  starting transfers between devices  7.46 us (3%)
    all_to_all x1, blocking collectives, local(): lax.all_to_all(outgoing, 'context', split_axis=0, concat_axis=0, tiled=True)  113 us
    reduce_scatter x1, waiting for transfers between devices, local(): lax.psum_scatter(partial_out.astype(jnp.bfloat16), 'tensor', scatter_dime...  61 us
    all_to_all x1, waiting for transfers between devices, local(): lax.all_to_all(expert_out, 'context', split_axis=0, concat_axis=0, tiled=...  17.3 us
    dot_general x1, matrix products, local(): jnp.dot(activated, w_down[0], preferred_element_type=jnp.float32)  7.88 us
    all_to_all x1, starting transfers between devices, local(): lax.all_to_all(expert_out, 'context', split_axis=0, concat_axis=0, tiled=...  7.46 us
  transfers between devices with their start and end apart: 2, of which 2 were waited for; matrix products, arithmetic and copies ran while one was open for 0% of the time, Pallas kernels for 0%

commit v1 on v0

v1 whole, which is shorter than its diff:
```python
import jax
import jax.numpy as jnp
from jax import lax
from jax.experimental import pallas as pl
from jax.experimental.pallas import tpu as pltpu
from jax.sharding import PartitionSpec as P

CAP = 32
CHIPS = 8
OFFSETS = (0, 1, 7, 2, 6, 3, 5, 4)
CHUNKS = ((0, 1, True), (1, 2, False), (3, 2, False), (5, 2, False), (7, 1, True))
PIECES = 2
ORDER = (
    ("Y", 0), ("Y", 1), ("W",), ("Y", 2), ("Y", 3), ("Y", 4),
    ("A", 0), ("B", 0), ("S", 0, 0), ("S", 0, 1), ("A", 1), ("S", 0, 2),
    ("B", 1), ("S", 1, 0), ("S", 0, 3), ("A", 2), ("S", 1, 1), ("F", 0),
    ("B", 2), ("S", 2, 0), ("S", 1, 2), ("S", 2, 1), ("A", 3), ("S", 1, 3),
    ("S", 2, 2), ("B", 3), ("S", 3, 0), ("F", 1), ("S", 2, 3), ("S", 3, 1),
    ("F", 2), ("A", 4), ("B", 4), ("S", 4, 0), ("S", 3, 2), ("S", 4, 1),
    ("S", 3, 3), ("S", 4, 2), ("F", 3), ("S", 4, 3), ("F", 4), ("C", 0),
    ("C", 1), ("C", 2), ("C", 3), ("C", 4),
)
BOTH_LAST = (((1,), (1,)), ((), ()))
BOTH_FIRST = (((0,), (0,)), ((), ()))
MESH = pl.DeviceIdType.MESH


def kernel(
    ids_ref, mix_ref, hidden_ref, gate_ref, up_ref, down_ref, out_ref,
    sel_ref, comb_ref, total_ref, hid, wg, wu, wd, outgoing, arrived, act, rs_out, rs_in, mixed_rows, returned,
    load_sem, y_send, y_recv, f_send, f_recv, r_send, r_recv, b_send, b_recv,
):
    ctx, z = lax.axis_index("context"), lax.axis_index("tensor")
    y, core = ctx // 2, ctx % 2
    width = hidden_ref.shape[1]
    half, quarter, block = width // 2, width // 4, width // 8
    own = pl.multiple_of((z % 2) * half, half)
    other = pl.multiple_of((1 - z % 2) * half, half)
    right, left = (z + 1) % CHIPS, (z + CHIPS - 1) % CHIPS

    loads = []
    for n, (source, begin) in enumerate(((own, 0), (other, half))):
        loads.append(
            pltpu.make_async_copy(
                hidden_ref.at[:, pl.ds(source, half)], hid.at[:, pl.ds(begin, half)],
                load_sem.at[n],
            )
        )
    for n, (source, begin) in enumerate(((own, 0), (other, half))):
        for m, (src, dst) in enumerate(((gate_ref, wg), (up_ref, wu))):
            loads.append(
                pltpu.make_async_copy(
                    src.at[0, :, pl.ds(source, half)], dst.at[:, pl.ds(begin, half)],
                    load_sem.at[2 + 2 * n + m],
                )
            )
    loads.append(pltpu.make_async_copy(down_ref.at[0], wd, load_sem.at[6]))
    for load in loads:
        load.start()

    def peer(dy, dc):
        return ((y + dy) % CHIPS) * 2 + (core + dc) % 2

    barrier = pltpu.get_barrier_semaphore()
    for dy in range(CHIPS):
        for dc in range(2):
            if dy or dc:
                pl.semaphore_signal(
                    barrier, inc=1, device_id={"context": peer(dy, dc)}, device_id_type=MESH
                )
    for side in (right, left):
        pl.semaphore_signal(barrier, inc=1, device_id={"tensor": side}, device_id_type=MESH)

    tokens = hidden_ref.shape[0]
    row = lax.broadcasted_iota(jnp.int32, (2 * CHIPS, tokens), 0)
    place = row // 2
    shift = jnp.zeros_like(place)
    for n, offset in enumerate(OFFSETS):
        shift = jnp.where(place == n, offset, shift)
    expert = ((y + shift) % CHIPS) * 2 + (core + row % 2) % 2
    chosen = jnp.zeros((2 * CHIPS, tokens), jnp.float32)
    weight = jnp.zeros((2 * CHIPS, tokens), jnp.float32)
    for n in range(ids_ref.shape[0]):
        match = ids_ref[n:n + 1, :] == expert
        chosen = jnp.where(match, 1.0, chosen)
        weight = jnp.where(match, mix_ref[n:n + 1, :], weight)
    before = (
        lax.broadcasted_iota(jnp.int32, (tokens, tokens), 0)
        <= lax.broadcasted_iota(jnp.int32, (tokens, tokens), 1)
    )
    count = jnp.dot(
        chosen.astype(jnp.bfloat16), jnp.where(before, 1.0, 0.0).astype(jnp.bfloat16),
        preferred_element_type=jnp.float32,
    )
    slot = jnp.where(chosen > 0.0, count - 1.0, -1.0)
    slot_ids = lax.broadcasted_iota(jnp.int32, (CAP, tokens), 0).astype(jnp.float32)
    for n in range(2 * CHIPS):
        sel_ref[n * CAP:(n + 1) * CAP, :] = jnp.where(
            slot[n:n + 1, :] == slot_ids, 1.0, 0.0
        ).astype(jnp.bfloat16)

    loads[0].wait()
    loads[1].wait()
    pl.semaphore_wait(barrier, 2 * CHIPS + 1)

    y_copies, forwards, sums, backs = {}, {}, {}, {}

    def extent(k):
        begin, count, whole = CHUNKS[k]
        return begin * 2 * CAP, (begin + count) * 2 * CAP, 4 if whole else 2

    def dispatch(k):
        low, top, quarters = extent(k)
        for q in range(quarters):
            picked = jnp.dot(
                sel_ref[low:top, :], hid[:, q * quarter:(q + 1) * quarter],
                preferred_element_type=jnp.float32,
            ).astype(jnp.bfloat16)
            outgoing[q, low:top, :] = picked
            if low == 0:
                arrived[q, 0:CAP, :] = picked[0:CAP]
        for n in range(low // CAP, top // CAP):
            if n == 0:
                continue
            piece = (pl.ds(0, quarters), pl.ds(CAP * n, CAP), slice(None))
            copy = pltpu.make_async_remote_copy(
                src_ref=outgoing.at[piece], dst_ref=arrived.at[piece],
                send_sem=y_send.at[n], recv_sem=y_recv.at[n],
                device_id={"context": peer(OFFSETS[n // 2], n % 2)}, device_id_type=MESH,
            )
            copy.start()
            y_copies[n] = copy

    def weigh():
        for n in range(2 * CHIPS):
            combiner = jnp.where(slot[n:n + 1, :] == slot_ids, weight[n:n + 1, :], 0.0)
            high = combiner.astype(jnp.bfloat16)
            comb_ref[0, n * CAP:(n + 1) * CAP, :] = high
            comb_ref[1, n * CAP:(n + 1) * CAP, :] = (
                combiner - high.astype(jnp.float32)
            ).astype(jnp.bfloat16)

    def arrive(k):
        low, top, quarters = extent(k)
        for n in range(low // CAP, top // CAP):
            if n:
                y_copies[n].wait_recv()
        if quarters == 4:
            return
        span = pl.ds(low, top - low)
        for side, to in enumerate((right, left)):
            copy = pltpu.make_async_remote_copy(
                src_ref=arrived.at[side, span, :], dst_ref=arrived.at[2 + side, span, :],
                send_sem=f_send.at[k, side], recv_sem=f_recv.at[k, side],
                device_id={"tensor": to}, device_id_type=MESH,
            )
            copy.start()
            forwards[k, side] = copy

    def expand(k):
        low, top, quarters = extent(k)
        if k == 0:
            for load in loads[2:]:
                load.wait()
        gate = up = None
        for q in range(4):
            if q >= quarters:
                forwards[k, q - 2].wait_recv()
            x = arrived[q, low:top, :]
            here = slice(q * quarter, (q + 1) * quarter)
            g = lax.dot_general(x, wg[:, here], BOTH_LAST, preferred_element_type=jnp.float32)
            u = lax.dot_general(x, wu[:, here], BOTH_LAST, preferred_element_type=jnp.float32)
            gate = g if gate is None else gate + g
            up = u if up is None else up + u
        act[low:top, :] = (gate / (1.0 + jnp.exp(-gate)) * up).astype(jnp.bfloat16)

    def part(k, target, begin, size):
        low, top, _ = extent(k)
        columns = pl.ds(pl.multiple_of(target * block + begin, size), size)
        return jnp.dot(act[low:top, :], wd[:, columns], preferred_element_type=jnp.float32)

    narrow = block // 2

    def step(k, s):
        low, top, _ = extent(k)
        size = (top - low) // PIECES
        totals = []
        for side in range(2):
            shift = 4 - s
            target = (z + shift) % CHIPS if side == 0 else (z + CHIPS - shift) % CHIPS
            if s == 0:
                totals.append(part(k, target, side * narrow, narrow))
            else:
                totals.append(part(k, target, 0, block))
        for piece in range(PIECES):
            begin, end = low + piece * size, low + (piece + 1) * size
            for side, to in enumerate((right, left)):
                total = totals[side][piece * size:(piece + 1) * size]
                if s:
                    sums[k, s - 1, side, piece].wait_recv()
                if s == 0:
                    rs_out[side, 0, begin:end, 0:narrow] = total.astype(jnp.bfloat16)
                elif s == 1:
                    mine = slice(side * narrow, (side + 1) * narrow)
                    rest = slice((1 - side) * narrow, (2 - side) * narrow)
                    rs_out[side, s, begin:end, mine] = (
                        total[:, mine] + rs_in[side, 0, begin:end, 0:narrow].astype(jnp.float32)
                    ).astype(jnp.bfloat16)
                    rs_out[side, s, begin:end, rest] = total[:, rest].astype(jnp.bfloat16)
                else:
                    total = total + rs_in[side, s - 1, begin:end, :].astype(jnp.float32)
                    rs_out[side, s, begin:end, :] = total.astype(jnp.bfloat16)
                place = (side, s, pl.ds(begin, size), pl.ds(0, block if s else narrow))
                copy = pltpu.make_async_remote_copy(
                    src_ref=rs_out.at[place], dst_ref=rs_in.at[place],
                    send_sem=r_send.at[k, s, side, piece], recv_sem=r_recv.at[k, s, side, piece],
                    device_id={"tensor": to}, device_id_type=MESH,
                )
                copy.start()
                sums[k, s, side, piece] = copy

    def finish(k):
        low, top, _ = extent(k)
        size = (top - low) // PIECES
        whole = part(k, z, 0, block)
        for piece in range(PIECES):
            begin, end = low + piece * size, low + (piece + 1) * size
            total = whole[piece * size:(piece + 1) * size]
            for side in range(2):
                sums[k, 3, side, piece].wait_recv()
                total = total + rs_in[side, 3, begin:end, :].astype(jnp.float32)
            total = total.astype(jnp.bfloat16)
            mixed_rows[begin:end, :] = total
            for n in range(begin // CAP, end // CAP):
                if n == 0:
                    returned[0:CAP, :] = total[0:CAP]
                    continue
                span = pl.ds(CAP * n, CAP)
                copy = pltpu.make_async_remote_copy(
                    src_ref=mixed_rows.at[span, :], dst_ref=returned.at[span, :],
                    send_sem=b_send.at[n], recv_sem=b_recv.at[n],
                    device_id={"context": peer(CHIPS - OFFSETS[n // 2], n % 2)},
                    device_id_type=MESH,
                )
                copy.start()
                backs[n] = copy

    def combine(k):
        low, top, _ = extent(k)
        for n in range(low // CAP, top // CAP):
            if n:
                backs[n].wait_recv()
        total = None if k == 0 else total_ref[...]
        for n in range(2):
            term = lax.dot_general(
                comb_ref[n, low:top, :], returned[low:top, :], BOTH_FIRST,
                preferred_element_type=jnp.float32,
            )
            total = term if total is None else total + term
        if k == len(CHUNKS) - 1:
            out_ref[...] = total.astype(out_ref.dtype)
        else:
            total_ref[...] = total

    tasks = {"Y": dispatch, "A": arrive, "B": expand, "S": step, "F": finish, "C": combine, "W": weigh}
    for task in ORDER:
        tasks[task[0]](*task[1:])

    for group in (y_copies, forwards, sums, backs):
        for copy in group.values():
            copy.wait_send()


def local(hidden, expert_ids, gate_weights, w_gate, w_up, w_down):
    tokens, width = hidden.shape
    units = w_gate.shape[2]
    block = width // CHIPS
    rows = 2 * CHIPS * CAP
    chunks = len(CHUNKS)
    bf16 = jnp.bfloat16
    vmem = pl.BlockSpec(memory_space=pltpu.VMEM)
    hbm = pl.BlockSpec(memory_space=pl.ANY)
    dma = pltpu.SemaphoreType.DMA
    return pl.pallas_call(
        kernel,
        out_shape=jax.ShapeDtypeStruct((tokens, block), bf16),
        in_specs=[vmem] * 2 + [hbm] * 4,
        out_specs=vmem,
        scratch_shapes=[
            pltpu.VMEM((rows, tokens), bf16),
            pltpu.VMEM((2, rows, tokens), bf16),
            pltpu.VMEM((tokens, block), jnp.float32),
            pltpu.VMEM((tokens, width), bf16),
            pltpu.VMEM((units, width), bf16),
            pltpu.VMEM((units, width), bf16),
            pltpu.VMEM((units, width), bf16),
            pltpu.VMEM((4, rows, width // 4), bf16),
            pltpu.VMEM((4, rows, width // 4), bf16),
            pltpu.VMEM((rows, units), bf16),
            pltpu.VMEM((2, 4, rows, block), bf16),
            pltpu.VMEM((2, 4, rows, block), bf16),
            pltpu.VMEM((rows, block), bf16),
            pltpu.VMEM((rows, block), bf16),
            dma((7,)),
            dma((16,)), dma((16,)),
            dma((chunks, 2)), dma((chunks, 2)),
            dma((chunks, 4, 2, PIECES)), dma((chunks, 4, 2, PIECES)),
            dma((16,)), dma((16,)),
        ],
        compiler_params=pltpu.CompilerParams(
            collective_id=0, has_side_effects=True, vmem_limit_bytes=60 << 20
        ),
    )(
        expert_ids.T, gate_weights.T, hidden, jnp.swapaxes(w_gate, 1, 2),
        jnp.swapaxes(w_up, 1, 2), w_down,
    )


def solution(mesh):
    placed = (
        P(("dp", "context"), None),
        P(("dp", "context"), None),
        P(("dp", "context"), None),
        P("context", None, "tensor"),
        P("context", None, "tensor"),
        P("context", "tensor", None),
    )
    return jax.shard_map(
        local, mesh=mesh, in_specs=placed, out_specs=P(("dp", "context"), "tensor"), check_vma=False
    )
```

time: 228 us -> 113 us (0.50)
  the two profiles are of different devices: /device:TPU:1 before, /device:TPU:44 now
where the time goes in v1:
time: 113 us
  Pallas kernels  112 us (99%)
  local copies, waits for them, and re-layouts  1.67 us (1%)
    pallas_call x1, Pallas kernels, local(): pl.pallas_call(kernel, out_shape=jax.ShapeDtypeStruct((tokens, block), bf...  112 us

profile of v1, /device:TPU:44, one launch (start us, length us, event | category | flops | bytes accessed | tf_op | source)
XLA Modules:
  0.0 113.3 jit_solution(4099645488055154782)
XLA Ops:
  0.0 111.6 %shard_map.64 = bf16[256,512]{1,0:T(8,128)(2,1)} custom-call(s32[8,256]{1,0:T(8,128)} %bitcast.6, f32[8,256]{1,0:T(8,128)} %bitcast.7, bf16[256,4096]{1,0:T(8,128)(2,1)} %hidden_ref.1, bf16[1,192,4096]{2,1,0:T(8,128)(2,1)} %bitcast.4, bf16[1,192,4096]{2,1,0:T(8,128)(2,1)} %bitcast.5, bf16[1,192,4096]{2,1,0:T(8,128)(2,1)} %down_ref.1), custom_call_target="tpu_custom_call" | custom-call | tf_op jit(solution)/shard_map/pallas_call | solution.py:284
  111.6 1.7 %copy.8 = bf16[256,512]{1,0:T(8,128)(2,1)} copy(bf16[256,512]{1,0:T(8,128)(2,1)} %shard_map.64) | data formatting | bytes 524288

commit v2 on v1

--- a/solution.py
+++ b/solution.py
@@ -7,18 +7,18 @@
 
 CAP = 32
 CHIPS = 8
-OFFSETS = (0, 1, 7, 2, 6, 3, 5, 4)
-CHUNKS = ((0, 1, True), (1, 2, False), (3, 2, False), (5, 2, False), (7, 1, True))
+OFFSETS = (0, 2, 6, 4, 3, 5, 1, 7)
+CHUNKS = ((0, 1, 8), (1, 2, 2), (3, 1, 2), (4, 2, 4), (6, 2, 8))
 PIECES = 2
 ORDER = (
     ("Y", 0), ("Y", 1), ("W",), ("Y", 2), ("Y", 3), ("Y", 4),
-    ("A", 0), ("B", 0), ("S", 0, 0), ("S", 0, 1), ("A", 1), ("S", 0, 2),
-    ("B", 1), ("S", 1, 0), ("S", 0, 3), ("A", 2), ("S", 1, 1), ("F", 0),
-    ("B", 2), ("S", 2, 0), ("S", 1, 2), ("S", 2, 1), ("A", 3), ("S", 1, 3),
-    ("S", 2, 2), ("B", 3), ("S", 3, 0), ("F", 1), ("S", 2, 3), ("S", 3, 1),
-    ("F", 2), ("A", 4), ("B", 4), ("S", 4, 0), ("S", 3, 2), ("S", 4, 1),
-    ("S", 3, 3), ("S", 4, 2), ("F", 3), ("S", 4, 3), ("F", 4), ("C", 0),
-    ("C", 1), ("C", 2), ("C", 3), ("C", 4),
+    ("A", 0), ("B", 0), ("S", 0, 0), ("S", 0, 1), ("S", 0, 2), ("A", 1),
+    ("S", 0, 3), ("G", 1), ("A", 2), ("F", 0), ("B", 1), ("S", 1, 0),
+    ("G", 2), ("S", 1, 1), ("B", 2), ("S", 2, 0), ("S", 1, 2), ("S", 2, 1),
+    ("A", 3), ("S", 2, 2), ("S", 1, 3), ("B", 3), ("S", 3, 0), ("S", 2, 3),
+    ("A", 4), ("B", 4), ("F", 1), ("S", 3, 1), ("S", 4, 0), ("F", 2),
+    ("S", 3, 2), ("S", 4, 1), ("S", 3, 3), ("S", 4, 2), ("F", 3), ("S", 4, 3),
+    ("F", 4), ("C", 0), ("C", 1), ("C", 2), ("C", 3), ("C", 4),
 )
 BOTH_LAST = (((1,), (1,)), ((), ()))
 BOTH_FIRST = (((0,), (0,)), ((), ()))
@@ -27,13 +27,15 @@
 
 def kernel(
     ids_ref, mix_ref, hidden_ref, gate_ref, up_ref, down_ref, out_ref,
-    sel_ref, comb_ref, total_ref, hid, wg, wu, wd, outgoing, arrived, act, rs_out, rs_in, mixed_rows, returned,
+    sel_ref, comb_ref, total_ref, hid, wg, wu, wd, outgoing, arrived, act,
+    rs_out, rs_in, mixed_rows, returned,
     load_sem, y_send, y_recv, f_send, f_recv, r_send, r_recv, b_send, b_recv,
 ):
     ctx, z = lax.axis_index("context"), lax.axis_index("tensor")
     y, core = ctx // 2, ctx % 2
     width = hidden_ref.shape[1]
     half, quarter, block = width // 2, width // 4, width // 8
+    turn = (z // 2) % 2
     own = pl.multiple_of((z % 2) * half, half)
     other = pl.multiple_of((1 - z % 2) * half, half)
     right, left = (z + 1) % CHIPS, (z + CHIPS - 1) % CHIPS
@@ -106,23 +108,25 @@
     y_copies, forwards, sums, backs = {}, {}, {}, {}
 
     def extent(k):
-        begin, count, whole = CHUNKS[k]
-        return begin * 2 * CAP, (begin + count) * 2 * CAP, 4 if whole else 2
+        begin, count, eighths = CHUNKS[k]
+        return begin * 2 * CAP, (begin + count) * 2 * CAP, eighths // 2
 
     def dispatch(k):
         low, top, quarters = extent(k)
         for q in range(quarters):
+            at = turn if quarters == 1 else q
+            columns = pl.ds(pl.multiple_of(at * quarter, quarter), quarter)
             picked = jnp.dot(
-                sel_ref[low:top, :], hid[:, q * quarter:(q + 1) * quarter],
+                sel_ref[low:top, :], hid[:, columns],
                 preferred_element_type=jnp.float32,
             ).astype(jnp.bfloat16)
-            outgoing[q, low:top, :] = picked
+            outgoing[at, low:top, :] = picked
             if low == 0:
                 arrived[q, 0:CAP, :] = picked[0:CAP]
         for n in range(low // CAP, top // CAP):
             if n == 0:
                 continue
-            piece = (pl.ds(0, quarters), pl.ds(CAP * n, CAP), slice(None))
+            piece = (pl.ds(turn if quarters == 1 else 0, quarters), pl.ds(CAP * n, CAP), slice(None))
             copy = pltpu.make_async_remote_copy(
                 src_ref=outgoing.at[piece], dst_ref=arrived.at[piece],
                 send_sem=y_send.at[n], recv_sem=y_recv.at[n],
@@ -149,22 +153,40 @@
             return
         span = pl.ds(low, top - low)
         for side, to in enumerate((right, left)):
+            at = turn if quarters == 1 else side
             copy = pltpu.make_async_remote_copy(
-                src_ref=arrived.at[side, span, :], dst_ref=arrived.at[2 + side, span, :],
+                src_ref=arrived.at[at, span, :], dst_ref=arrived.at[2 + at, span, :],
                 send_sem=f_send.at[k, side], recv_sem=f_recv.at[k, side],
                 device_id={"tensor": to}, device_id_type=MESH,
             )
             copy.start()
             forwards[k, side] = copy
 
+    def relay(k):
+        low, top, _ = extent(k)
+        for side, to in enumerate((right, left)):
+            at = ((left if side == 0 else right) // 2) % 2
+            forwards[k, side].wait_recv()
+            place = (pl.ds(low, top - low), pl.ds(side * block, block))
+            copy = pltpu.make_async_remote_copy(
+                src_ref=arrived.at[(2 + at,) + place], dst_ref=arrived.at[(at,) + place],
+                send_sem=f_send.at[k, 2 + side], recv_sem=f_recv.at[k, 2 + side],
+                device_id={"tensor": to}, device_id_type=MESH,
+            )
+            copy.start()
+            forwards[k, 2 + side] = copy
+
     def expand(k):
         low, top, quarters = extent(k)
+        if quarters == 1:
+            for side in range(2):
+                forwards[k, 2 + side].wait_recv()
         if k == 0:
             for load in loads[2:]:
                 load.wait()
         gate = up = None
         for q in range(4):
-            if q >= quarters:
+            if quarters == 2 and q >= 2:
                 forwards[k, q - 2].wait_recv()
             x = arrived[q, low:top, :]
             here = slice(q * quarter, (q + 1) * quarter)
@@ -262,7 +284,10 @@
         else:
             total_ref[...] = total
 
-    tasks = {"Y": dispatch, "A": arrive, "B": expand, "S": step, "F": finish, "C": combine, "W": weigh}
+    tasks = {
+        "Y": dispatch, "A": arrive, "G": relay, "B": expand, "S": step, "F": finish,
+        "C": combine, "W": weigh,
+    }
     for task in ORDER:
         tasks[task[0]](*task[1:])
 
@@ -303,7 +328,7 @@
             pltpu.VMEM((rows, block), bf16),
             dma((7,)),
             dma((16,)), dma((16,)),
-            dma((chunks, 2)), dma((chunks, 2)),
+            dma((chunks, 4)), dma((chunks, 4)),
             dma((chunks, 4, 2, PIECES)), dma((chunks, 4, 2, PIECES)),
             dma((16,)), dma((16,)),
         ],

time: 113 us -> 103 us (0.912)
  the two profiles are of different devices: /device:TPU:44 before, /device:TPU:1 now
where the time goes in v2:
time: 103 us; the launch traced here: 102 us
  Pallas kernels  101 us (98%)
  local copies, waits for them, and re-layouts  1.67 us (2%)
    pallas_call x1, Pallas kernels, local(): pl.pallas_call(kernel, out_shape=jax.ShapeDtypeStruct((tokens, block), bf...  101 us

profile of v2, /device:TPU:1, one launch (start us, length us, event | category | flops | bytes accessed | tf_op | source)
XLA Modules:
  0.0 102.4 jit_solution(4631871517171752626)
XLA Ops:
  0.0 100.8 %shard_map.64 = bf16[256,512]{1,0:T(8,128)(2,1)} custom-call(s32[8,256]{1,0:T(8,128)} %bitcast.6, f32[8,256]{1,0:T(8,128)} %bitcast.7, bf16[256,4096]{1,0:T(8,128)(2,1)} %hidden_ref.1, bf16[1,192,4096]{2,1,0:T(8,128)(2,1)} %bitcast.4, bf16[1,192,4096]{2,1,0:T(8,128)(2,1)} %bitcast.5, bf16[1,192,4096]{2,1,0:T(8,128)(2,1)} %down_ref.1), custom_call_target="tpu_custom_call" | custom-call | tf_op jit(solution)/shard_map/pallas_call | solution.py:309
  100.8 1.7 %copy.8 = bf16[256,512]{1,0:T(8,128)(2,1)} copy(bf16[256,512]{1,0:T(8,128)(2,1)} %shard_map.64) | data formatting | bytes 524288

commit v3 on v2

--- a/solution.py
+++ b/solution.py
@@ -11,14 +11,15 @@
 CHUNKS = ((0, 1, 8), (1, 2, 2), (3, 1, 2), (4, 2, 4), (6, 2, 8))
 PIECES = 2
 ORDER = (
-    ("Y", 0), ("Y", 1), ("W",), ("Y", 2), ("Y", 3), ("Y", 4),
-    ("A", 0), ("B", 0), ("S", 0, 0), ("S", 0, 1), ("S", 0, 2), ("A", 1),
-    ("S", 0, 3), ("G", 1), ("A", 2), ("F", 0), ("B", 1), ("S", 1, 0),
-    ("G", 2), ("S", 1, 1), ("B", 2), ("S", 2, 0), ("S", 1, 2), ("S", 2, 1),
-    ("A", 3), ("S", 2, 2), ("S", 1, 3), ("B", 3), ("S", 3, 0), ("S", 2, 3),
-    ("A", 4), ("B", 4), ("F", 1), ("S", 3, 1), ("S", 4, 0), ("F", 2),
-    ("S", 3, 2), ("S", 4, 1), ("S", 3, 3), ("S", 4, 2), ("F", 3), ("S", 4, 3),
-    ("F", 4), ("C", 0), ("C", 1), ("C", 2), ("C", 3), ("C", 4),
+    ("Y", 1), ("Y", 0), ("A", 0), ("B", 0), ("D", 0), ("S", 0, 0),
+    ("Y", 2), ("S", 0, 1), ("S", 0, 2), ("W",), ("A", 1), ("Y", 3),
+    ("S", 0, 3), ("G", 1), ("A", 2), ("Y", 4), ("F", 0), ("B", 1),
+    ("D", 1), ("S", 1, 0), ("G", 2), ("S", 1, 1), ("B", 2), ("D", 2),
+    ("S", 2, 0), ("S", 1, 2), ("S", 2, 1), ("A", 3), ("S", 2, 2), ("S", 1, 3),
+    ("B", 3), ("D", 3), ("S", 3, 0), ("S", 2, 3), ("A", 4), ("B", 4),
+    ("D", 4), ("F", 1), ("S", 3, 1), ("S", 4, 0), ("F", 2), ("S", 3, 2),
+    ("S", 4, 1), ("S", 3, 3), ("S", 4, 2), ("F", 3), ("S", 4, 3), ("F", 4),
+    ("C", 0), ("C", 1), ("C", 2), ("C", 3), ("C", 4),
 )
 BOTH_LAST = (((1,), (1,)), ((), ()))
 BOTH_FIRST = (((0,), (0,)), ((), ()))
@@ -40,26 +41,6 @@
     other = pl.multiple_of((1 - z % 2) * half, half)
     right, left = (z + 1) % CHIPS, (z + CHIPS - 1) % CHIPS
 
-    loads = []
-    for n, (source, begin) in enumerate(((own, 0), (other, half))):
-        loads.append(
-            pltpu.make_async_copy(
-                hidden_ref.at[:, pl.ds(source, half)], hid.at[:, pl.ds(begin, half)],
-                load_sem.at[n],
-            )
-        )
-    for n, (source, begin) in enumerate(((own, 0), (other, half))):
-        for m, (src, dst) in enumerate(((gate_ref, wg), (up_ref, wu))):
-            loads.append(
-                pltpu.make_async_copy(
-                    src.at[0, :, pl.ds(source, half)], dst.at[:, pl.ds(begin, half)],
-                    load_sem.at[2 + 2 * n + m],
-                )
-            )
-    loads.append(pltpu.make_async_copy(down_ref.at[0], wd, load_sem.at[6]))
-    for load in loads:
-        load.start()
-
     def peer(dy, dc):
         return ((y + dy) % CHIPS) * 2 + (core + dc) % 2
 
@@ -72,6 +53,26 @@
                 )
     for side in (right, left):
         pl.semaphore_signal(barrier, inc=1, device_id={"tensor": side}, device_id_type=MESH)
+
+    loads = []
+    for n, (source, begin) in enumerate(((own, 0), (other, half))):
+        loads.append(
+            pltpu.make_async_copy(
+                hidden_ref.at[:, pl.ds(source, half)], hid.at[:, pl.ds(begin, half)],
+                load_sem.at[n],
+            )
+        )
+    for n, (source, begin) in enumerate(((own, 0), (other, half))):
+        for m, (src, dst) in enumerate(((gate_ref, wg), (up_ref, wu))):
+            loads.append(
+                pltpu.make_async_copy(
+                    src.at[0, :, pl.ds(source, half)], dst.at[:, pl.ds(begin, half)],
+                    load_sem.at[2 + 2 * n + m],
+                )
+            )
+    loads.append(pltpu.make_async_copy(down_ref.at[0], wd, load_sem.at[6]))
+    for load in loads:
+        load.start()
 
     tokens = hidden_ref.shape[0]
     row = lax.broadcasted_iota(jnp.int32, (2 * CHIPS, tokens), 0)
@@ -176,24 +177,32 @@
             copy.start()
             forwards[k, 2 + side] = copy
 
+    halves = {}
+
+    def multiply(k, quarters):
+        low, top, _ = extent(k)
+        for q in quarters:
+            x = arrived[q, low:top, :]
+            here = slice(q * quarter, (q + 1) * quarter)
+            terms = [
+                lax.dot_general(x, w[:, here], BOTH_LAST, preferred_element_type=jnp.float32)
+                for w in (wg, wu)
+            ]
+            halves[k] = [a + b for a, b in zip(halves[k], terms)] if k in halves else terms
+
     def expand(k):
-        low, top, quarters = extent(k)
-        if quarters == 1:
-            for side in range(2):
-                forwards[k, 2 + side].wait_recv()
         if k == 0:
             for load in loads[2:]:
                 load.wait()
-        gate = up = None
-        for q in range(4):
-            if quarters == 2 and q >= 2:
-                forwards[k, q - 2].wait_recv()
-            x = arrived[q, low:top, :]
-            here = slice(q * quarter, (q + 1) * quarter)
-            g = lax.dot_general(x, wg[:, here], BOTH_LAST, preferred_element_type=jnp.float32)
-            u = lax.dot_general(x, wu[:, here], BOTH_LAST, preferred_element_type=jnp.float32)
-            gate = g if gate is None else gate + g
-            up = u if up is None else up + u
+        multiply(k, (2, 3) if extent(k)[2] == 1 else (0, 1))
+
+    def activate(k):
+        low, top, quarters = extent(k)
+        if quarters < 4:
+            for side in range(2):
+                forwards[k, side + (2 if quarters == 1 else 0)].wait_recv()
+        multiply(k, (0, 1) if quarters == 1 else (2, 3))
+        gate, up = halves.pop(k)
         act[low:top, :] = (gate / (1.0 + jnp.exp(-gate)) * up).astype(jnp.bfloat16)
 
     def part(k, target, begin, size):
@@ -285,7 +294,7 @@
             total_ref[...] = total
 
     tasks = {
-        "Y": dispatch, "A": arrive, "G": relay, "B": expand, "S": step, "F": finish,
+        "Y": dispatch, "A": arrive, "G": relay, "B": expand, "D": activate, "S": step, "F": finish,
         "C": combine, "W": weigh,
     }
     for task in ORDER:

time: 103 us -> 101 us (0.981)
  Pallas kernels: 101 us -> 98.3 us
    pallas_call x1, Pallas kernels: 101 us -> 98.3 us  [local(): pl.pallas_call(kernel, out_shape=jax.ShapeDtypeStruct((tokens, block), bf...]
where the time goes in v3:
time: 101 us; the launch traced here: 100 us
  Pallas kernels  98.3 us (97%)
  local copies, waits for them, and re-layouts  1.67 us (2%)
    pallas_call x1, Pallas kernels, local(): pl.pallas_call(kernel, out_shape=jax.ShapeDtypeStruct((tokens, block), bf...  98.3 us

profile of v3, /device:TPU:1, one launch (start us, length us, event | category | flops | bytes accessed | tf_op | source)
XLA Modules:
  0.0 100.0 jit_solution(16498998568157589898)
XLA Ops:
  0.0 98.3 %shard_map.64 = bf16[256,512]{1,0:T(8,128)(2,1)} custom-call(s32[8,256]{1,0:T(8,128)} %bitcast.6, f32[8,256]{1,0:T(8,128)} %bitcast.7, bf16[256,4096]{1,0:T(8,128)(2,1)} %hidden_ref.1, bf16[1,192,4096]{2,1,0:T(8,128)(2,1)} %bitcast.4, bf16[1,192,4096]{2,1,0:T(8,128)(2,1)} %bitcast.5, bf16[1,192,4096]{2,1,0:T(8,128)(2,1)} %down_ref.1), custom_call_target="tpu_custom_call" | custom-call | tf_op jit(solution)/shard_map/pallas_call | solution.py:318
  98.3 1.7 %copy.8 = bf16[256,512]{1,0:T(8,128)(2,1)} copy(bf16[256,512]{1,0:T(8,128)(2,1)} %shard_map.64) | data formatting | bytes 524288

commit v4 on v3

--- a/solution.py
+++ b/solution.py
@@ -28,13 +28,13 @@
 
 def kernel(
     ids_ref, mix_ref, hidden_ref, gate_ref, up_ref, down_ref, out_ref,
-    sel_ref, comb_ref, total_ref, hid, wg, wu, wd, outgoing, arrived, act,
+    sel_ref, comb_ref, total_ref, hid, pair, wd, outgoing, arrived, act,
     rs_out, rs_in, mixed_rows, returned,
     load_sem, y_send, y_recv, f_send, f_recv, r_send, r_recv, b_send, b_recv,
 ):
     ctx, z = lax.axis_index("context"), lax.axis_index("tensor")
     y, core = ctx // 2, ctx % 2
-    width = hidden_ref.shape[1]
+    width, units = hidden_ref.shape[1], gate_ref.shape[1]
     half, quarter, block = width // 2, width // 4, width // 8
     turn = (z // 2) % 2
     own = pl.multiple_of((z % 2) * half, half)
@@ -63,10 +63,11 @@
             )
         )
     for n, (source, begin) in enumerate(((own, 0), (other, half))):
-        for m, (src, dst) in enumerate(((gate_ref, wg), (up_ref, wu))):
+        for m, src in enumerate((gate_ref, up_ref)):
             loads.append(
                 pltpu.make_async_copy(
-                    src.at[0, :, pl.ds(source, half)], dst.at[:, pl.ds(begin, half)],
+                    src.at[0, :, pl.ds(source, half)],
+                    pair.at[pl.ds(m * units, units), pl.ds(begin, half)],
                     load_sem.at[2 + 2 * n + m],
                 )
             )
@@ -184,11 +185,10 @@
         for q in quarters:
             x = arrived[q, low:top, :]
             here = slice(q * quarter, (q + 1) * quarter)
-            terms = [
-                lax.dot_general(x, w[:, here], BOTH_LAST, preferred_element_type=jnp.float32)
-                for w in (wg, wu)
-            ]
-            halves[k] = [a + b for a, b in zip(halves[k], terms)] if k in halves else terms
+            term = lax.dot_general(
+                x, pair[:, here], BOTH_LAST, preferred_element_type=jnp.float32
+            )
+            halves[k] = halves[k] + term if k in halves else term
 
     def expand(k):
         if k == 0:
@@ -202,7 +202,8 @@
             for side in range(2):
                 forwards[k, side + (2 if quarters == 1 else 0)].wait_recv()
         multiply(k, (0, 1) if quarters == 1 else (2, 3))
-        gate, up = halves.pop(k)
+        total = halves.pop(k)
+        gate, up = total[:, 0:units], total[:, units:2 * units]
         act[low:top, :] = (gate / (1.0 + jnp.exp(-gate)) * up).astype(jnp.bfloat16)
 
     def part(k, target, begin, size):
@@ -325,8 +326,7 @@
             pltpu.VMEM((2, rows, tokens), bf16),
             pltpu.VMEM((tokens, block), jnp.float32),
             pltpu.VMEM((tokens, width), bf16),
-            pltpu.VMEM((units, width), bf16),
-            pltpu.VMEM((units, width), bf16),
+            pltpu.VMEM((2 * units, width), bf16),
             pltpu.VMEM((units, width), bf16),
             pltpu.VMEM((4, rows, width // 4), bf16),
             pltpu.VMEM((4, rows, width // 4), bf16),

time: 101 us -> 101 us (level)
  no operation moved by 1% of the time
where the time goes in v4:
time: 101 us; the launch traced here: 100 us
  Pallas kernels  98.7 us (98%)
  local copies, waits for them, and re-layouts  1.67 us (2%)
    pallas_call x1, Pallas kernels, local(): pl.pallas_call(kernel, out_shape=jax.ShapeDtypeStruct((tokens, block), bf...  98.7 us

profile of v4, /device:TPU:1, one launch (start us, length us, event | category | flops | bytes accessed | tf_op | source)
XLA Modules:
  0.0 100.4 jit_solution(13771547525668777706)
XLA Ops:
  0.0 98.7 %shard_map.64 = bf16[256,512]{1,0:T(8,128)(2,1)} custom-call(s32[8,256]{1,0:T(8,128)} %bitcast.6, f32[8,256]{1,0:T(8,128)} %bitcast.7, bf16[256,4096]{1,0:T(8,128)(2,1)} %hidden_ref.1, bf16[1,192,4096]{2,1,0:T(8,128)(2,1)} %bitcast.4, bf16[1,192,4096]{2,1,0:T(8,128)(2,1)} %bitcast.5, bf16[1,192,4096]{2,1,0:T(8,128)(2,1)} %down_ref.1), custom_call_target="tpu_custom_call" | custom-call | tf_op jit(solution)/shard_map/pallas_call | solution.py:319
  98.8 1.7 %copy.8 = bf16[256,512]{1,0:T(8,128)(2,1)} copy(bf16[256,512]{1,0:T(8,128)(2,1)} %shard_map.64) | data formatting | bytes 524288
